TPU v7x, 512 devices: a whole 4x4x16 slice. The times are simulated.
512 devices in a mesh: wide: 128 (over z_lo, x, y, core), narrow: 4 (over z_hi).
Axes of the slice: x: 4, y: 4, z: 16 (z_hi: 4, z_lo: 4; z = z_hi * 4 + z_lo), core: 2. Of those that a mesh axis runs over, the one named last changes fastest.
Arguments:
- grad_in: float32 [131072, 128], P(('wide', 'narrow')), may hold values from -6 to 6
- phi_slope: bfloat16 [131072, 128], P(('wide', 'narrow')), may hold values from 0.049804688 to 1
- activations: bfloat16 [131072, 128], P(('wide', 'narrow')), may hold values from -6 to 6
- weight: bfloat16 [128, 128], replicated, may hold values from -0.5 to 0.5
- local_tiles: bfloat16 [512, 8, 128, 128], P(('wide', 'narrow')), may hold values from -0.0625 to 0.0625
- local_rows: int32 [512, 8], P(('wide', 'narrow')), may hold values from 0 to 1, as said below
- local_cols: int32 [512, 8], P(('wide', 'narrow')), may hold values from 0 to 7, as said below
- local_count: int32 [512], P(('wide', 'narrow')), may hold values from 1 to 8, 3072 in all
- remote_tiles: bfloat16 [512, 112, 128, 128], P(('wide', 'narrow')), may hold values from -0.0625 to 0.0625
- remote_rows: int32 [512, 112], P(('wide', 'narrow')), may hold values from 0 to 1, as said below
- remote_cols: int32 [512, 112], P(('wide', 'narrow')), may hold values from 0 to 55, as said below
- remote_count: int32 [512], P(('wide', 'narrow')), may hold values from 1 to 112, 43008 in all
- send_list: int32 [512, 128, 56], P(('wide', 'narrow')), may hold values from 0 to 1023
Outputs:
- adjoint: float32 [131072, 128], P(('wide', 'narrow'))
- weight_grad: float32 [128, 128], replicated
Inputs may be any that keep to these rules, and one draw needn't show every extreme that they name: `local_count`: each device's live local tile slots; slots from this count onward are ignored, and some device uses all 8. `remote_count`: each device's live remote tile slots; slots from this count onward are ignored, and some device uses all 112. On one device no two local slots have the same pair of local_rows and local_cols. `local_cols`: see local_rows. On one device no two remote slots have the same pair of remote_rows and remote_cols. `remote_cols`: see remote_rows.
All inputs are finite; a program needn't handle non-finite values.
Results may differ from a plain program's by a relative error of at most 0.0031.
Values may be sent and summed in bfloat16 or wider, within the bound.
A program may use at most 64 MiB of HBM per device.

v0:
```python
import jax
import jax.numpy as jnp
from jax import lax
from jax.sharding import PartitionSpec as P

ITERS = 2
GAMMA = 0.5


def row_table(row_ids, live_count, blocks):
    slot_count = row_ids.shape[0]
    is_live = jnp.arange(slot_count, dtype=jnp.int32) < live_count
    matches = row_ids[None, :] == jnp.arange(blocks, dtype=jnp.int32)[:, None]
    return (matches & is_live[None, :]).astype(jnp.float32)


def tile_product(tile_values, table, picked, hidden):
    product = jnp.einsum("kij,kjh->kih", tile_values, picked, preferred_element_type=jnp.float32)
    summed = jnp.einsum("rk,kih->rih", table, product, precision=lax.Precision.HIGHEST)
    return summed.reshape(-1, hidden)


def per_device(
    grad_in,
    phi_slope,
    activations,
    weight,
    local_tiles,
    local_rows,
    local_cols,
    local_count,
    remote_tiles,
    remote_rows,
    remote_cols,
    remote_count,
    send_list,
):
    dev_rows = grad_in.shape[0]
    hidden = grad_in.shape[1]
    tile_size = local_tiles.shape[2]
    blocks = dev_rows // tile_size
    group_blocks = lax.axis_size("narrow") * blocks
    near_table = row_table(local_rows[0], local_count[0], blocks)
    far_table = row_table(remote_rows[0], remote_count[0], blocks)
    all_tiles = jnp.concatenate([local_tiles[0], remote_tiles[0]], axis=0)
    all_table = jnp.concatenate([near_table, far_table], axis=1)
    all_cols = jnp.concatenate([local_cols[0], remote_cols[0] + group_blocks], axis=0)
    adjoint = grad_in
    for iteration in range(ITERS):
        mapped = jnp.einsum(
            "nk,hk->nh", adjoint.astype(jnp.bfloat16), weight, preferred_element_type=jnp.float32
        )
        message = (mapped * phi_slope).astype(jnp.bfloat16)
        gathered = lax.all_gather(message, "narrow", axis=0, tiled=True)
        outgoing = gathered[send_list[0]]
        incoming = lax.all_to_all(outgoing, "wide", split_axis=0, concat_axis=0, tiled=True)
        halo_blocks = incoming.reshape(-1, tile_size, hidden)
        own_blocks = gathered.reshape(-1, tile_size, hidden)
        sources = jnp.concatenate([own_blocks, halo_blocks], axis=0)
        spread = tile_product(all_tiles, all_table, sources[all_cols], hidden)
        adjoint = grad_in + GAMMA * spread
    partial_sum = lax.dot_general(
        activations,
        adjoint.astype(jnp.bfloat16),
        (((0,), (0,)), ((), ())),
        preferred_element_type=jnp.float32,
    )
    summed = lax.psum(partial_sum, ("wide", "narrow"))
    node_total = dev_rows * lax.axis_size("wide") * lax.axis_size("narrow")
    weight_grad = summed * (GAMMA / jnp.sqrt(jnp.float32(node_total)))
    return (adjoint, weight_grad)


def solution(mesh):
    placed = (
        P(("wide", "narrow"), None),
        P(("wide", "narrow"), None),
        P(("wide", "narrow"), None),
        P(),
        P(("wide", "narrow"), None, None, None),
        P(("wide", "narrow"), None),
        P(("wide", "narrow"), None),
        P(("wide", "narrow")),
        P(("wide", "narrow"), None, None, None),
        P(("wide", "narrow"), None),
        P(("wide", "narrow"), None),
        P(("wide", "narrow")),
        P(("wide", "narrow"), None, None),
    )
    return jax.shard_map(
        per_device,
        mesh=mesh,
        in_specs=placed,
        out_specs=(P(("wide", "narrow"), None), P()),
        check_vma=False,
    )
```

profile of v0, /device:TPU:1, one launch (start us, length us, event | category | flops | bytes accessed | tf_op | source)
XLA Modules:
  0.0 687.4 jit_solution(18382776733626664124)
XLA Ops:
  7.2 1.1 fusion.12
  8.3 25.3 %all_gather.6 = bf16[1024,128]{1,0:T(8,128)(2,1)S(1)} all-gather(bf16[256,128]{1,0:T(8,128)(2,1)S(1)} %fusion.12), channel_id=1, replica_groups=mesh['wide'=128,'narrow'=4] {'narrow'}, dimensions={0}, use_global_device_ids=true | all-gather | bytes 327680 | tf_op jit(solution)/shard_map/all_gather | solution.py:54
  33.6 0.8 compare_select_fusion
  34.6 25.5 %gather_fusion = bf16[7168,128]{1,0:T(8,128)(2,1)} fusion(bf16[1024,128]{1,0:T(8,128)(2,1)S(1)} %all_gather.6, s32[7168]{0:T(1024)S(1)} %broadcast_clamp_fusion), kind=kCustom, calls=%fused_computation | custom fusion | bytes 3698688 | tf_op jit(solution)/shard_map/gather | solution.py:55
  60.1 13.1 %all-to-all-start = ((bf16[128,56,128]{2,1,0:T(8,128)(2,1)}), bf16[128,56,128]{2,1,0:T(8,128)(2,1)S(1)}, u32[]{:S(2)}, u32[]{:S(2)}) async-start(bf16[128,56,128]{2,1,0:T(8,128)(2,1)} %bitcast.47), calls=%async_computation | async-start | bytes 3670016 | tf_op jit(solution)/shard_map/all_to_all | solution.py:56
  73.3 0.2 all-reduce.2.cloned.1.call-start
  75.0 44.7 %all-to-all-done = bf16[128,56,128]{2,1,0:T(8,128)(2,1)S(1)} async-done(((bf16[128,56,128]{2,1,0:T(8,128)(2,1)}), bf16[128,56,128]{2,1,0:T(8,128)(2,1)S(1)}, u32[]{:S(2)}, u32[]{:S(2)}) %all-to-all-start) | async-done | bytes 1835040 | tf_op jit(solution)/shard_map/all_to_all | solution.py:56
  119.7 1.3 copy-done.1
  120.9 1.7 pad_maximum_fusion.3
  122.6 2.9 gather_fusion.1
  125.6 4.4 fusion.5
  130.0 7.1 %fusion.6 = f32[2,128,128]{2,0,1:T(2,128)S(1)} fusion(f32[120,128,128]{2,1,0:T(8,128)S(1)} %fusion.5, pred[2,112]{1,0:T(4,128)(4,1)S(1)} %compare_and_fusion, pred[2,8]{1,0:T(4,128)(4,1)S(1)} %compare_and_fusion.1), kind=kOutput, calls=%fused_computation.13 | convolution fusion | flops 47218928 | bytes 7995632 | tf_op jit(solution)/shard_map/rk,kih->rih/dot_general | solution.py:19
  137.2 0.2 fusion.13
  137.3 18.3 %all_gather.7 = bf16[1024,128]{1,0:T(8,128)(2,1)S(1)} all-gather(bf16[256,128]{1,0:T(8,128)(2,1)S(1)} %fusion.13), channel_id=1, replica_groups=mesh['wide'=128,'narrow'=4] {'narrow'}, dimensions={0}, use_global_device_ids=true | all-gather | bytes 327680 | tf_op jit(solution)/shard_map/all_gather | solution.py:54
  155.6 21.1 %gather_fusion.2 = bf16[7168,128]{1,0:T(8,128)(2,1)S(1)} fusion(bf16[1024,128]{1,0:T(8,128)(2,1)S(1)} %all_gather.7, s32[7168]{0:T(1024)S(1)} %broadcast_clamp_fusion), kind=kCustom, calls=%fused_computation.2 | custom fusion | bytes 3698688 | tf_op jit(solution)/shard_map/gather | solution.py:55
  176.7 53.7 %all_to_all.10 = bf16[128,56,128]{2,1,0:T(8,128)(2,1)S(1)} all-to-all(bf16[128,56,128]{2,1,0:T(8,128)(2,1)S(1)} %bitcast.48), channel_id=1, replica_groups=mesh['wide'=128,'narrow'=4] {'wide'}, dimensions={0} | all-to-all | bytes 3670016 | tf_op jit(solution)/shard_map/all_to_all | solution.py:56
  230.3 0.2 pad_maximum_fusion.4
  230.5 2.9 gather_fusion.3
  233.4 4.4 fusion.4
  237.9 7.1 %fusion.9 = f32[2,128,128]{2,0,1:T(2,128)S(1)} fusion(f32[120,128,128]{2,1,0:T(8,128)S(1)} %fusion.4, pred[2,112]{1,0:T(4,128)(4,1)S(1)} %compare_and_fusion, pred[2,8]{1,0:T(4,128)(4,1)S(1)} %compare_and_fusion.1), kind=kOutput, calls=%fused_computation.14 | convolution fusion | flops 47218928 | bytes 7995632 | tf_op jit(solution)/shard_map/rk,kih->rih/dot_general | solution.py:19
  245.0 0.8 convolution_bitcast_fusion
  245.8 433.1 %all-reduce.2.cloned.1.call-done = f32[128,128]{0,1:T(8,128)} async-done(((f32[128,128]{0,1:T(8,128)}), f32[128,128]{0,1:T(8,128)}) %all-reduce.2.cloned.1.call-update) | async-done | bytes 65552 | tf_op jit(solution)/shard_map/psum | solution.py:68
  679.0 0.8 broadcast_multiply_fusion
  679.8 0.7 copy.19
  (36 shorter events, 0.5 us)
Async XLA Ops:
  7.2 237.8 %copy-start = (bf16[256,128]{1,0:T(8,128)(2,1)S(1)}, bf16[256,128]{1,0:T(8,128)(2,1)}, u32[]{:S(2)}) copy-start(bf16[256,128]{1,0:T(8,128)(2,1)} %param.15) | copy-start | bytes 196612
  34.5 40.3 %copy-start.7 = (s32[1,112]{1,0:T(1,128)S(1)}, s32[1,112]{1,0:T(1,128)}, u32[]{:S(2)}) copy-start(s32[1,112]{1,0:T(1,128)} %param.23) | copy-start | bytes 1348
  34.5 40.3 %copy-start.8 = (s32[1,8]{1,0:T(1,128)S(1)}, s32[1,8]{1,0:T(1,128)}, u32[]{:S(2)}) copy-start(s32[1,8]{1,0:T(1,128)} %param.19) | copy-start | bytes 100
  34.6 40.4 %copy-start.9 = (s32[1,112]{1,0:T(1,128)S(1)}, s32[1,112]{1,0:T(1,128)}, u32[]{:S(2)}) copy-start(s32[1,112]{1,0:T(1,128)} %param.22) | copy-start | bytes 1348
  34.6 40.4 %copy-start.10 = (s32[1,8]{1,0:T(1,128)S(1)}, s32[1,8]{1,0:T(1,128)}, u32[]{:S(2)}) copy-start(s32[1,8]{1,0:T(1,128)} %param.18) | copy-start | bytes 100
  60.1 59.5 %all-to-all-start = ((bf16[128,56,128]{2,1,0:T(8,128)(2,1)}), bf16[128,56,128]{2,1,0:T(8,128)(2,1)S(1)}, u32[]{:S(2)}, u32[]{:S(2)}) async-start(bf16[128,56,128]{2,1,0:T(8,128)(2,1)} %bitcast.47), calls=%async_computation | async-start | bytes 3670016 | tf_op jit(solution)/shard_map/all_to_all | solution.py:56
  73.3 605.7 %all-reduce.2.cloned.1.call-start = ((), (), s32[]{:S(2)}) async-start(), calls=%async_computation.2 | async-start | bytes 131072 | tf_op jit(solution)/shard_map/psum | solution.py:68
  119.7 1.3 copy-start.1
  122.6 2.9 copy-start.3
  130.0 7.1 %copy-start.2 = (f32[256,128]{1,0:T(8,128)S(1)}, f32[256,128]{1,0:T(8,128)}, u32[]{:S(2)}) copy-start(f32[256,128]{1,0:T(8,128)} %param.13) | copy-start | bytes 393220
  130.0 7.1 %copy-start.5 = (bf16[256,128]{1,0:T(8,128)(2,1)S(1)}, bf16[256,128]{1,0:T(8,128)(2,1)}, u32[]{:S(2)}) copy-start(bf16[256,128]{1,0:T(8,128)(2,1)} %param.14) | copy-start | bytes 196612
  130.0 7.1 %copy-start.6 = (bf16[128,128]{1,0:T(8,128)(2,1)S(1)}, bf16[128,128]{1,0:T(8,128)(2,1)}, u32[]{:S(2)}) copy-start(bf16[128,128]{1,0:T(8,128)(2,1)} %param.16) | copy-start | bytes 98308
  245.0 435.6 %copy-start.4 = (f32[256,128]{1,0:T(8,128)}, f32[256,128]{1,0:T(8,128)S(1)}, u32[]{:S(2)}) copy-start(f32[256,128]{1,0:T(8,128)S(1)} %bitcast_add_fusion) | copy-start | bytes 393220
Sparse Core Ops, SparseCore 0:
  245.9 432.9 all-reduce.1
where the time goes:
time: 688 us; the launch traced here: 687 us
  waiting for transfers between devices  478 us (69%)
  blocking collectives  97.2 us (14%)
  local copies, waits for them, and re-layouts  54.7 us (8%)
  matrix products  25.1 us (4%)
  between operations  15.6 us (2%)
  starting transfers between devices  13.4 us (2%)
    psum x1, waiting for transfers between devices, per_device(): summed = lax.psum(partial_sum, ('wide', 'narrow'))  433 us
    all_to_all x1, blocking collectives, per_device(): lax.all_to_all(outgoing, 'wide', split_axis=0, concat_axis=0, tiled=True)  53.7 us
    gather x2, local copies, waits for them, and re-layouts, per_device(): outgoing = gathered[send_list[0]]  46.6 us
    all_to_all x1, waiting for transfers between devices, per_device(): lax.all_to_all(outgoing, 'wide', split_axis=0, concat_axis=0, tiled=True)  44.7 us
    all_gather x2, blocking collectives, per_device(): gathered = lax.all_gather(message, 'narrow', axis=0, tiled=True)  43.5 us
    dot_general x2, matrix products, tile_product(): jnp.einsum('rk,kih->rih', table, product, precision=lax.Precision.HIGHEST)  14.1 us
  transfers between devices with their start and end apart: 2, of which 2 were waited for; matrix products, arithmetic and copies ran while one was open for 0% of the time, Pallas kernels for 0%

commit v1 on v0

--- a/solution.py
+++ b/solution.py
@@ -65,7 +65,8 @@
         (((0,), (0,)), ((), ())),
         preferred_element_type=jnp.float32,
     )
-    summed = lax.psum(partial_sum, ("wide", "narrow"))
+    handle_stacks_all = lambda sample, a_name: jnp.sum(lax.all_gather(sample, a_name), axis=0)
+    summed = handle_stacks_all(partial_sum, ("wide", "narrow"))
     node_total = dev_rows * lax.axis_size("wide") * lax.axis_size("narrow")
     weight_grad = summed * (GAMMA / jnp.sqrt(jnp.float32(node_total)))
     return (adjoint, weight_grad)

time: 688 us -> 1460 us (2.12)
  waiting for transfers between devices: 478 us -> 1230 us
  local copies, waits for them, and re-layouts: 54.7 us -> 72.1 us
    all_gather x0 -> x1, waiting for transfers between devices: none -> 1180 us  [per_device(): lax.all_gather(sample, a_name)]
    psum x1 -> x0, waiting for transfers between devices: 433 us -> none  [per_device(): summed = lax.psum(partial_sum, ('wide', 'narrow'))]
    unnamed x23 -> x26, local copies, waits for them, and re-layouts: 2.06 us -> 19.3 us
where the time goes in v1:
time: 1460 us
  waiting for transfers between devices  1230 us (84%)
  blocking collectives  97 us (7%)
  local copies, waits for them, and re-layouts  72.1 us (5%)
  matrix products  25 us (2%)
  between operations  15.6 us (1%)
    all_gather x1, waiting for transfers between devices, per_device(): lax.all_gather(sample, a_name)  1180 us
    all_to_all x1, blocking collectives, per_device(): lax.all_to_all(outgoing, 'wide', split_axis=0, concat_axis=0, tiled=True)  53.5 us
    gather x2, local copies, waits for them, and re-layouts, per_device(): outgoing = gathered[send_list[0]]  46.8 us
    all_to_all x1, waiting for transfers between devices, per_device(): lax.all_to_all(outgoing, 'wide', split_axis=0, concat_axis=0, tiled=True)  44.7 us
    all_gather x2, blocking collectives, per_device(): gathered = lax.all_gather(message, 'narrow', axis=0, tiled=True)  43.5 us
  transfers between devices with their start and end apart: 2, of which 2 were waited for; matrix products, arithmetic and copies ran while one was open for 0% of the time, Pallas kernels for 0%

profile of v1, /device:TPU:1, one launch (start us, length us, event | category | flops | bytes accessed | tf_op | source)
XLA Modules:
  0.0 1459.0 jit_solution(4785702120035647469)
XLA Ops:
  7.2 0.8 compare_select_fusion
  8.2 1.1 fusion.12
  9.3 25.3 %all_gather.12 = bf16[1024,128]{1,0:T(8,128)(2,1)S(1)} all-gather(bf16[256,128]{1,0:T(8,128)(2,1)S(1)} %fusion.12), channel_id=1, replica_groups=mesh['wide'=128,'narrow'=4] {'narrow'}, dimensions={0}, use_global_device_ids=true | all-gather | bytes 327680 | tf_op jit(solution)/shard_map/all_gather | solution.py:54
  34.6 25.7 %gather_fusion = bf16[7168,128]{1,0:T(8,128)(2,1)} fusion(bf16[1024,128]{1,0:T(8,128)(2,1)S(1)} %all_gather.12, s32[7168]{0:T(1024)S(1)} %broadcast_clamp_fusion), kind=kCustom, calls=%fused_computation | custom fusion | bytes 3698688 | tf_op jit(solution)/shard_map/gather | solution.py:55
  60.3 13.1 all-to-all-start
  73.4 0.2 all-gather.3.cloned.1.call-start
  75.1 44.7 %all-to-all-done = bf16[128,56,128]{2,1,0:T(8,128)(2,1)S(1)} async-done(((bf16[128,56,128]{2,1,0:T(8,128)(2,1)}), bf16[128,56,128]{2,1,0:T(8,128)(2,1)S(1)}, u32[]{:S(2)}, u32[]{:S(2)}) %all-to-all-start) | async-done | bytes 1835040 | tf_op jit(solution)/shard_map/all_to_all | solution.py:56
  119.8 1.3 copy-done.2
  121.1 1.7 pad_maximum_fusion.3
  122.8 2.9 gather_fusion.1
  125.7 4.4 fusion.5
  130.2 7.1 fusion.6
  137.5 18.2 %all_gather.13 = bf16[1024,128]{1,0:T(8,128)(2,1)S(1)} all-gather(bf16[256,128]{1,0:T(8,128)(2,1)S(1)} %fusion.13), channel_id=1, replica_groups=mesh['wide'=128,'narrow'=4] {'narrow'}, dimensions={0}, use_global_device_ids=true | all-gather | bytes 327680 | tf_op jit(solution)/shard_map/all_gather | solution.py:54
  155.7 21.1 %gather_fusion.2 = bf16[7168,128]{1,0:T(8,128)(2,1)S(1)} fusion(bf16[1024,128]{1,0:T(8,128)(2,1)S(1)} %all_gather.13, s32[7168]{0:T(1024)S(1)} %broadcast_clamp_fusion), kind=kCustom, calls=%fused_computation.2 | custom fusion | bytes 3698688 | tf_op jit(solution)/shard_map/gather | solution.py:55
  176.8 53.5 %all_to_all.10 = bf16[128,56,128]{2,1,0:T(8,128)(2,1)S(1)} all-to-all(bf16[128,56,128]{2,1,0:T(8,128)(2,1)S(1)} %bitcast.54), channel_id=1, replica_groups=mesh['wide'=128,'narrow'=4] {'wide'}, dimensions={0} | all-to-all | bytes 3670016 | tf_op jit(solution)/shard_map/all_to_all | solution.py:56
  230.3 0.2 pad_maximum_fusion.4
  230.5 2.9 gather_fusion.3
  233.4 4.4 fusion.4
  237.8 7.1 fusion.9
  245.0 0.8 convolution_bitcast_fusion
  245.8 1184.4 %all-gather.3.cloned.1.call-done = f32[65536,128]{0,1:T(8,128)} async-done(((f32[128,128]{0,1:T(8,128)}), f32[65536,128]{0,1:T(8,128)}) %all-gather.3.cloned.1.call-update) | async-done | bytes 33554448 | tf_op jit(solution)/shard_map/all_gather | solution.py:68
  1430.2 17.2 %copy.24 = f32[16,8,512,128]{3,2,1,0:T(8,128)S(1)} copy(f32[16,8,512,128]{3,1,2,0:T(8,128)} %bitcast.48) | data formatting | bytes 67108864
  1447.4 4.0 bitcast_reduce_fusion
  1451.4 0.7 copy.23
  (40 shorter events, 0.6 us)
Async XLA Ops:
  7.2 237.8 %copy-start = (bf16[256,128]{1,0:T(8,128)(2,1)S(1)}, bf16[256,128]{1,0:T(8,128)(2,1)}, u32[]{:S(2)}) copy-start(bf16[256,128]{1,0:T(8,128)(2,1)} %param.15) | copy-start | bytes 196612
  34.5 40.4 %copy-start.8 = (s32[1,112]{1,0:T(1,128)S(1)}, s32[1,112]{1,0:T(1,128)}, u32[]{:S(2)}) copy-start(s32[1,112]{1,0:T(1,128)} %param.23) | copy-start | bytes 1348
  34.5 40.4 %copy-start.9 = (s32[1,8]{1,0:T(1,128)S(1)}, s32[1,8]{1,0:T(1,128)}, u32[]{:S(2)}) copy-start(s32[1,8]{1,0:T(1,128)} %param.19) | copy-start | bytes 100
  34.5 40.5 %copy-start.10 = (s32[1,112]{1,0:T(1,128)S(1)}, s32[1,112]{1,0:T(1,128)}, u32[]{:S(2)}) copy-start(s32[1,112]{1,0:T(1,128)} %param.22) | copy-start | bytes 1348
  34.5 40.6 %copy-start.11 = (s32[1,8]{1,0:T(1,128)S(1)}, s32[1,8]{1,0:T(1,128)}, u32[]{:S(2)}) copy-start(s32[1,8]{1,0:T(1,128)} %param.18) | copy-start | bytes 100
  60.3 59.5 %all-to-all-start = ((bf16[128,56,128]{2,1,0:T(8,128)(2,1)}), bf16[128,56,128]{2,1,0:T(8,128)(2,1)S(1)}, u32[]{:S(2)}, u32[]{:S(2)}) async-start(bf16[128,56,128]{2,1,0:T(8,128)(2,1)} %bitcast.53), calls=%async_computation | async-start | bytes 3670016 | tf_op jit(solution)/shard_map/all_to_all | solution.py:56
  73.4 1356.8 %all-gather.3.cloned.1.call-start = ((), (), s32[]{:S(2)}) async-start(), calls=%async_computation.2 | async-start | bytes 33619968 | tf_op jit(solution)/shard_map/all_gather | solution.py:68
  119.8 1.3 copy-start.2
  122.8 2.9 copy-start.4
  130.1 7.1 copy-start.3
  130.2 7.1 copy-start.6
  130.2 7.1 copy-start.7
  245.0 1202.5 %copy-start.5 = (f32[256,128]{1,0:T(8,128)}, f32[256,128]{1,0:T(8,128)S(1)}, u32[]{:S(2)}) copy-start(f32[256,128]{1,0:T(8,128)S(1)} %bitcast_add_fusion) | copy-start | bytes 393220
  1447.4 4.7 copy-start.1
Sparse Core Ops, SparseCore 0:
  245.9 1184.2 all-gather.2
